TPU v7x, 32 devices: a whole 2x2x4 slice. The times are simulated.
32 devices in a mesh: expert: 8 (over y, x, core), dp: 4 (over z).
Axes of the slice: x: 2, y: 2, z: 4, core: 2. Of those that a mesh axis runs over, the one named last changes fastest.
Arguments:
- tokens: bfloat16 [4096, 2048], P(('expert', 'dp')), may hold values from -6 to 6
- cotangent: bfloat16 [4096, 2048], P(('expert', 'dp')), may hold values from -4 to 4
- expert_ids: int32 [4096, 8], P('expert'), may hold values from 0 to 31, all different within a row; in each aligned block of 512 rows (0 to 511, 512 to 1023, ...) at most 160 rows name the same one
- router_probs: float32 [4096, 8], P('expert'), may hold values from 0.02 to 1
- w_gate: bfloat16 [32, 2048, 768], P(('expert', 'dp')), may hold values from -0.125 to 0.125
- w_up: bfloat16 [32, 2048, 768], P(('expert', 'dp')), may hold values from -0.125 to 0.125
- w_down: bfloat16 [32, 768, 2048], P(('expert', 'dp')), may hold values from -0.21875 to 0.21875
Outputs:
- moe_out: bfloat16 [4096, 2048], P(('expert', 'dp'))
- token_grad: bfloat16 [4096, 2048], P(('expert', 'dp'))
- prob_grad: float32 [4096, 8], P(('expert', 'dp'))
Inputs may be any that keep to these rules, and one draw needn't show every extreme that they name: `expert_ids`: each row names 8 different experts. In each aligned block of 512 rows (the tokens of one index of expert) no expert is named by more than 160 rows, and in some block one expert is named by exactly 160 rows.
All inputs are finite; a program needn't handle non-finite values.
Results may differ from a plain program's by a relative error of at most 0.0095.
Values may be sent and summed in bfloat16 or wider, within the bound.
A program may use at most 128 MiB of HBM per device.

v0:
```python
import jax
import jax.numpy as jnp
from jax import lax
from jax.sharding import PartitionSpec as P


def shards(tokens, cotangent, expert_ids, router_probs, w_gate, w_up, w_down):
    col_count = lax.axis_size("expert")
    group_count = lax.axis_size("dp")
    my_group = lax.axis_index("dp")
    tok_local = tokens.shape[0]
    width = tokens.shape[1]
    col_tokens = expert_ids.shape[0]
    top_count = expert_ids.shape[1]
    capacity = col_tokens * top_count * 5 // (4 * col_count * group_count)
    slot_count = col_count * capacity
    flat_count = col_tokens * top_count
    gate_matrix = w_gate[0]
    up_matrix = w_up[0]
    down_matrix = w_down[0]
    hidden_width = gate_matrix.shape[1]
    prob_total = jnp.sum(router_probs, axis=1, keepdims=True)
    weights = router_probs / prob_total
    expert_flat = expert_ids.reshape(-1)
    weight_flat = weights.reshape(-1)
    is_mine = expert_flat % group_count == my_group
    dest_column = expert_flat // group_count
    one_hot = jnp.logical_and(
        dest_column[:, None] == jnp.arange(col_count, dtype=jnp.int32)[None, :], is_mine[:, None]
    ).astype(jnp.int32)
    position = jnp.cumsum(one_hot, axis=0, dtype=jnp.int32) - 1
    slot_index = jnp.sum(position * one_hot, axis=1, dtype=jnp.int32)
    target = jnp.where(is_mine, dest_column * capacity + slot_index, slot_count)
    slot_row = (
        jnp.zeros((slot_count + 1,), jnp.int32)
        .at[target]
        .set(jnp.arange(flat_count, dtype=jnp.int32))[:slot_count]
    )
    filled = jnp.zeros((slot_count + 1,), jnp.float32).at[target].set(1.0)[:slot_count]
    slot_token = slot_row // top_count
    slot_weight = weight_flat[slot_row] * filled
    column = lax.all_gather(tokens, "dp", axis=0, tiled=True)
    picked = jnp.where(filled[:, None] > 0, column[slot_token], jnp.zeros((), jnp.bfloat16))
    token_rows = lax.all_to_all(
        picked.reshape(col_count, capacity, width),
        "expert",
        split_axis=0,
        concat_axis=0,
        tiled=True,
    )
    item_count = token_rows.shape[1]
    flat_rows = token_rows.reshape(-1, width)
    gate_pre = jnp.dot(flat_rows, gate_matrix, preferred_element_type=jnp.float32)
    up_pre = jnp.dot(flat_rows, up_matrix, preferred_element_type=jnp.float32)
    hidden = (jax.nn.silu(gate_pre) * up_pre).astype(jnp.bfloat16)
    expert_out = jnp.dot(hidden, down_matrix, preferred_element_type=jnp.float32).astype(
        jnp.bfloat16
    )
    expert_out, gate_pre, up_pre = (expert_out, gate_pre, up_pre)
    expert_out, gate_kept, up_kept = (
        expert_out.reshape(col_count, item_count, width),
        gate_pre.reshape(col_count, item_count, hidden_width),
        up_pre.reshape(col_count, item_count, hidden_width),
    )
    returned = lax.all_to_all(expert_out, "expert", split_axis=0, concat_axis=0, tiled=True)
    returned_flat = returned.reshape(slot_count, width)
    out_sum = lax.psum_scatter(
        jnp.zeros((col_tokens, width), jnp.float32)
        .at[slot_token]
        .add(slot_weight[:, None] * returned_flat.astype(jnp.float32))
        .astype(jnp.bfloat16),
        "dp",
        scatter_dimension=0,
        tiled=True,
    )
    cot_column = lax.all_gather(cotangent, "dp", axis=0, tiled=True)
    scaled = slot_weight[:, None] * cot_column[slot_token].astype(jnp.float32)
    cot_arrived = lax.all_to_all(
        scaled.astype(jnp.bfloat16).reshape(col_count, capacity, width),
        "expert",
        split_axis=0,
        concat_axis=0,
        tiled=True,
    )
    gate_pre = gate_kept.reshape(-1, hidden_width)
    hidden_grad = lax.dot_general(
        cot_arrived.reshape(-1, width),
        down_matrix,
        (((1,), (1,)), ((), ())),
        preferred_element_type=jnp.float32,
    )
    sigmoid_gate = jax.nn.sigmoid(gate_pre)
    gate_grad = (
        hidden_grad
        * up_kept.reshape(-1, hidden_width)
        * sigmoid_gate
        * (1.0 + gate_pre * (1.0 - sigmoid_gate))
    ).astype(jnp.bfloat16)
    up_grad = (hidden_grad * gate_pre * sigmoid_gate).astype(jnp.bfloat16)
    input_rows = lax.dot_general(
        gate_grad, gate_matrix, (((1,), (1,)), ((), ())), preferred_element_type=jnp.float32
    )
    input_rows = input_rows + lax.dot_general(
        up_grad, up_matrix, (((1,), (1,)), ((), ())), preferred_element_type=jnp.float32
    )
    input_rows = input_rows.astype(jnp.bfloat16)
    grad_rows = lax.all_to_all(
        input_rows.reshape(col_count, capacity, width),
        "expert",
        split_axis=0,
        concat_axis=0,
        tiled=True,
    )
    returned_flat = returned.reshape(slot_count, width)
    slot_grad = jnp.einsum(
        "rd,rd->r", cot_column[slot_token], returned_flat, preferred_element_type=jnp.float32
    )
    grad_flat = grad_rows.reshape(slot_count, width)
    grad_sum = lax.psum_scatter(
        jnp.zeros((col_tokens, width), jnp.float32)
        .at[slot_token]
        .add(grad_flat.astype(jnp.float32))
        .astype(jnp.bfloat16),
        "dp",
        scatter_dimension=0,
        tiled=True,
    )
    slot_sum = lax.psum_scatter(
        jnp.zeros((flat_count,), jnp.float32)
        .at[slot_row]
        .add(slot_grad)
        .reshape(col_tokens, top_count)
        .astype(jnp.bfloat16),
        "dp",
        scatter_dimension=0,
        tiled=True,
    ).astype(jnp.float32)
    own_weights = lax.dynamic_slice_in_dim(weights, my_group * tok_local, tok_local, 0)
    own_total = lax.dynamic_slice_in_dim(prob_total, my_group * tok_local, tok_local, 0)
    prob_grad = (slot_sum - jnp.sum(own_weights * slot_sum, axis=1, keepdims=True)) / own_total
    return (out_sum, grad_sum, prob_grad)


def solution(mesh):
    return jax.shard_map(
        shards,
        mesh=mesh,
        in_specs=(
            P(("expert", "dp"), None),
            P(("expert", "dp"), None),
            P("expert", None),
            P("expert", None),
            P(("expert", "dp"), None, None),
            P(("expert", "dp"), None, None),
            P(("expert", "dp"), None, None),
        ),
        out_specs=(P(("expert", "dp"), None), P(("expert", "dp"), None), P(("expert", "dp"), None)),
        check_vma=False,
    )
```

profile of v0, /device:TPU:0, one launch (start us, length us, event | category | flops | bytes accessed | tf_op | source)
XLA Modules:
  0.0 421.4 jit_solution(6338957533608779255)
XLA Ops:
  9.5 2.3 reduce-window.6
  12.8 15.5 %scatter_custom_fusion = s32[1281]{0:T(1024)S(1)} fusion(s32[4096]{0:T(1024)S(1)} %bitcast.54, s32[4096]{0:T(1024)S(1)} %iota.11, s32[]{:T(128)} %constant.37.clone.1), kind=kCustom, calls=%fused_computation.96 | custom fusion | bytes 5128 | tf_op jit(solution)/shard_map/scatter | solution.py:37
  28.3 15.5 %scatter_custom_fusion.1 = f32[1281]{0:T(1024)S(1)} fusion(s32[4096]{0:T(1024)S(1)} %bitcast.55, f32[4096]{0:T(1024)S(1)} %broadcast.241, f32[]{:T(128)} %constant.36.clone.1), kind=kCustom, calls=%fused_computation.94 | custom fusion | bytes 5128 | tf_op jit(solution)/shard_map/scatter | solution.py:39
  44.0 14.3 %all-gather.3.cloned.1.call-done = bf16[512,2048]{1,0:T(8,128)(2,1)} async-done(((bf16[128,2048]{1,0:T(8,128)(2,1)}), bf16[512,2048]{1,0:T(8,128)(2,1)}) %all-gather.3.cloned.1.call-update) | async-done | bytes 2097168 | tf_op jit(solution)/shard_map/all_gather | solution.py:42
  58.3 12.7 %gather_fusion.1 = bf16[1280,2048]{1,0:T(8,128)(2,1)} fusion(bf16[512,2048]{1,0:T(8,128)(2,1)} %all-gather.3.cloned.1.call-done, s32[2048]{0:T(1024)S(1)} %pad_clamp_fusion), kind=kCustom, calls=%fused_computation.1 | custom fusion | bytes 10490880 | tf_op jit(solution)/shard_map/gather | solution.py:43
  70.9 5.3 %broadcast_select_fusion = bf16[8,160,2048]{2,1,0:T(8,128)(2,1)} fusion(bf16[8,160,2048]{2,1,0:T(8,128)(2,1)} %bitcast.49, pred[8,160]{1,0:T(8,128)(4,1)S(1)} %gt.13), kind=kLoop, calls=%fused_computation.19 | loop fusion | flops 2621440 | bytes 10487040 | tf_op jit(solution)/shard_map/jit(_where)/select_n | solution.py:43
  76.2 4.8 %all-to-all-start = ((bf16[8,160,2048]{2,1,0:T(8,128)(2,1)}), bf16[8,160,2048]{2,1,0:T(8,128)(2,1)}, u32[]{:S(2)}, u32[]{:S(2)}) async-start(bf16[8,160,2048]{2,1,0:T(8,128)(2,1)} %broadcast_select_fusion), calls=%async_computation | async-start | bytes 10485760 | tf_op jit(solution)/shard_map/all_to_all | solution.py:44
  83.9 7.1 %gather_fusion = f32[1280]{0:T(1024)S(1)} fusion(f32[4096]{0:T(1024)S(1)} %reshape.235, s32[2048]{0:T(1024)S(1)} %pad_clamp_fusion.1), kind=kCustom, calls=%fused_computation | custom fusion | bytes 15360 | tf_op jit(solution)/shard_map/gather | solution.py:41
  91.0 37.4 %all-gather.5.cloned.1.call-done = bf16[512,2048]{1,0:T(8,128)(2,1)} async-done(((bf16[128,2048]{1,0:T(8,128)(2,1)}), bf16[512,2048]{1,0:T(8,128)(2,1)}) %all-gather.5.cloned.1.call-update) | async-done | bytes 2097168 | tf_op jit(solution)/shard_map/all_gather | solution.py:76
  128.5 12.7 %gather_fusion.2 = bf16[1280,2048]{1,0:T(8,128)(2,1)} fusion(bf16[512,2048]{1,0:T(8,128)(2,1)} %all-gather.5.cloned.1.call-done, s32[2048]{0:T(1024)S(1)} %pad_clamp_fusion), kind=kCustom, calls=%fused_computation.2 | custom fusion | bytes 10490880 | tf_op jit(solution)/shard_map/gather | solution.py:77
  141.2 5.6 %fusion.4 = bf16[8,160,2048]{2,1,0:T(8,128)(2,1)} fusion(bf16[8,160,2048]{2,1,0:T(8,128)(2,1)} %bitcast.48, f32[8,160]{1,0:T(8,128)S(1)} %mul.80), kind=kLoop, calls=%fused_computation.15 | loop fusion | flops 7864320 | bytes 10490880 | tf_op jit(solution)/shard_map/convert_element_type | solution.py:79
  146.8 4.8 %all-to-all-start.2 = ((bf16[8,160,2048]{2,1,0:T(8,128)(2,1)}), bf16[8,160,2048]{2,1,0:T(8,128)(2,1)}, u32[]{:S(2)}, u32[]{:S(2)}) async-start(bf16[8,160,2048]{2,1,0:T(8,128)(2,1)} %fusion.4), calls=%async_computation.3 | async-start | bytes 10485760 | tf_op jit(solution)/shard_map/all_to_all | solution.py:78
  151.7 7.3 %fusion.14 = f32[1280,768]{1,0:T(8,128)S(1)} fusion(bf16[1280,2048]{1,0:T(8,128)(2,1)} %bitcast.4, bf16[1,2048,768]{2,1,0:T(8,128)(2,1)} %param.11), kind=kOutput, calls=%fused_computation.32 | convolution fusion | flops 4026531840 | bytes 12320768 | tf_op jit(solution)/shard_map/dot_general | solution.py:53
  158.9 7.6 %fusion.10 = f32[1280,768]{1,0:T(8,128)S(1)} fusion(bf16[1280,2048]{1,0:T(8,128)(2,1)} %bitcast.4, bf16[1,2048,768]{2,1,0:T(8,128)(2,1)S(1)} %copy-done.3), kind=kOutput, calls=%fused_computation.28 | convolution fusion | flops 4026531840 | bytes 12320768 | tf_op jit(solution)/shard_map/dot_general | solution.py:54
  166.6 1.9 copy-done.8
  168.5 6.0 %convolution_convert_fusion = bf16[1280,2048]{1,0:T(8,128)(2,1)} fusion(bf16[1,768,2048]{2,1,0:T(8,128)(2,1)S(1)} %copy-done, f32[1280,768]{1,0:T(8,128)S(1)} %fusion.10, f32[1280,768]{1,0:T(8,128)S(1)} %fusion.14), kind=kOutput, calls=%fused_computation.17 | convolution fusion | flops 4035051520 | bytes 16252928 | tf_op jit(solution)/shard_map/dot_general | solution.py:56
  174.5 37.5 %all-to-all-done.2 = bf16[8,160,2048]{2,1,0:T(8,128)(2,1)} async-done(((bf16[8,160,2048]{2,1,0:T(8,128)(2,1)}), bf16[8,160,2048]{2,1,0:T(8,128)(2,1)}, u32[]{:S(2)}, u32[]{:S(2)}) %all-to-all-start.2) | async-done | bytes 5242912 | tf_op jit(solution)/shard_map/all_to_all | solution.py:78
  212.0 4.6 %all-to-all-start.1 = ((bf16[8,160,2048]{2,1,0:T(8,128)(2,1)}), bf16[8,160,2048]{2,1,0:T(8,128)(2,1)}, u32[]{:S(2)}, u32[]{:S(2)}) async-start(bf16[8,160,2048]{2,1,0:T(8,128)(2,1)} %bitcast.51), calls=%async_computation.1 | async-start | bytes 10485760 | tf_op jit(solution)/shard_map/all_to_all | solution.py:65
  216.7 6.4 %fusion.6 = f32[1280,768]{1,0:T(8,128)S(1)} fusion(bf16[1280,2048]{1,0:T(8,128)(2,1)} %bitcast.11, bf16[1,768,2048]{2,1,0:T(8,128)(2,1)S(1)} %copy-done), kind=kOutput, calls=%fused_computation.24 | convolution fusion | flops 4026531840 | bytes 12320768 | tf_op jit(solution)/shard_map/dot_general | solution.py:86
  223.1 1.9 copy-done.7
  225.0 9.1 %fusion.12 = f32[1280,2048]{1,0:T(8,128)} fusion(bf16[1,2048,768]{2,1,0:T(8,128)(2,1)S(1)} %copy-done.2, f32[1280,768]{1,0:T(8,128)S(1)} %copy-done.6, f32[1280,768]{1,0:T(8,128)S(1)} %fusion.6, f32[1280,768]{1,0:T(8,128)S(1)} %copy-done.9), kind=kOutput, calls=%fused_computation.30 | convolution fusion | flops 4036362240 | bytes 25427968 | tf_op jit(solution)/shard_map/dot_general | solution.py:100
  234.1 10.2 %add_convert_fusion = bf16[1280,2048]{1,0:T(8,128)(2,1)} fusion(f32[1280,2048]{1,0:T(8,128)} %fusion.12, bf16[1,2048,768]{2,1,0:T(8,128)(2,1)S(1)} %copy-done.4, f32[1280,768]{1,0:T(8,128)} %copy-done.7, f32[1280,768]{1,0:T(8,128)S(1)} %copy-done.6), kind=kOutput, calls=%fused_computation.16 | convolution fusion | flops 4037672960 | bytes 26738688 | tf_op jit(solution)/shard_map/dot_general | solution.py:103
  244.3 32.7 %all-to-all-done.1 = bf16[8,160,2048]{2,1,0:T(8,128)(2,1)} async-done(((bf16[8,160,2048]{2,1,0:T(8,128)(2,1)}), bf16[8,160,2048]{2,1,0:T(8,128)(2,1)}, u32[]{:S(2)}, u32[]{:S(2)}) %all-to-all-start.1) | async-done | bytes 5242912 | tf_op jit(solution)/shard_map/all_to_all | solution.py:65
  277.0 4.6 %all-to-all-start.3 = ((bf16[8,160,2048]{2,1,0:T(8,128)(2,1)}), bf16[8,160,2048]{2,1,0:T(8,128)(2,1)}, u32[]{:S(2)}, u32[]{:S(2)}) async-start(bf16[8,160,2048]{2,1,0:T(8,128)(2,1)} %bitcast.50), calls=%async_computation.4 | async-start | bytes 10485760 | tf_op jit(solution)/shard_map/all_to_all | solution.py:107
  281.9 5.5 %fusion.1 = f32[1280]{0:T(1024)S(1)} fusion(bf16[1280,2048]{1,0:T(8,128)(2,1)} %gather_fusion.2, bf16[8,160,2048]{2,1,0:T(8,128)(2,1)} %all-to-all-done.1), kind=kLoop, calls=%fused_computation.11 | loop fusion | flops 10484480 | bytes 10490880 | tf_op jit(solution)/shard_map/rd,rd->r/dot_general | solution.py:115
  287.4 9.3 %scatter_custom_fusion.4 = f32[4096]{0:T(1024)S(1)} fusion(s32[1280]{0:T(1024)S(1)} %get-tuple-element.6, f32[1280]{0:T(1024)S(1)} %fusion.1, f32[]{:T(128)} %constant.36.clone.1), kind=kCustom, calls=%fused_computation.88 | custom fusion | flops 1280 | bytes 16388 | tf_op jit(solution)/shard_map/scatter-add | solution.py:131
  297.6 23.8 %scatter_custom_fusion.2 = f32[512,2048]{1,0:T(8,128)} fusion(s32[1280]{0:T(1024)S(1)} %get-tuple-element.7, bf16[1280,2048]{1,0:T(8,128)(2,1)} %bitcast.9, f32[1280]{0:T(1024)S(1)} %slice_multiply_fusion, f32[]{:T(128)} %constant.36.clone.1), kind=kCustom, calls=%fused_computation.10 | custom fusion | flops 7864320 | bytes 9445380 | tf_op jit(solution)/shard_map/scatter-add | solution.py:70
  321.4 3.8 convert_element_type.59
  325.6 16.5 %all-to-all-done.3 = bf16[8,160,2048]{2,1,0:T(8,128)(2,1)} async-done(((bf16[8,160,2048]{2,1,0:T(8,128)(2,1)}), bf16[8,160,2048]{2,1,0:T(8,128)(2,1)}, u32[]{:S(2)}, u32[]{:S(2)}) %all-to-all-start.3) | async-done | bytes 5242912 | tf_op jit(solution)/shard_map/all_to_all | solution.py:107
  342.0 23.4 %scatter_custom_fusion.3 = f32[512,2048]{1,0:T(8,128)} fusion(s32[1280]{0:T(1024)S(1)} %get-tuple-element.7, bf16[1280,2048]{1,0:T(8,128)(2,1)} %bitcast.15, f32[]{:T(128)} %constant.36.clone.1), kind=kCustom, calls=%fused_computation.12 | custom fusion | flops 5242880 | bytes 9437188 | tf_op jit(solution)/shard_map/scatter-add | solution.py:122
  365.4 3.9 convert_element_type.68
  371.8 42.6 %reduce-scatter.6.cloned.1.call-done = bf16[128,2048]{1,0:T(8,128)(2,1)} async-done(((bf16[512,2048]{1,0:T(8,128)(2,1)}), bf16[128,2048]{1,0:T(8,128)(2,1)}) %reduce-scatter.6.cloned.1.call-update) | async-done | bytes 524304 | tf_op jit(solution)/shard_map/reduce_scatter | solution.py:119
  (64 shorter events, 10.2 us)
Async XLA Ops:
  7.2 161.3 %copy-start = (bf16[1,768,2048]{2,1,0:T(8,128)(2,1)S(1)}, bf16[1,768,2048]{2,1,0:T(8,128)(2,1)}, u32[]{:S(2)}) copy-start(bf16[1,768,2048]{2,1,0:T(8,128)(2,1)} %param.13) | copy-start | bytes 9437188
  7.2 51.1 %all-gather.3.cloned.1.call-start = ((), (), s32[]{:S(2)}) async-start(), calls=%async_computation.7 | async-start | bytes 2621440 | tf_op jit(solution)/shard_map/all_gather | solution.py:42
  76.2 5.5 %copy-start.1 = (f32[512,8]{0,1:T(8,128)S(1)}, f32[512,8]{0,1:T(8,128)}, u32[]{:S(2)}) copy-start(f32[512,8]{0,1:T(8,128)} %param.10) | copy-start | bytes 49156
  76.2 70.6 %all-to-all-start = ((bf16[8,160,2048]{2,1,0:T(8,128)(2,1)}), bf16[8,160,2048]{2,1,0:T(8,128)(2,1)}, u32[]{:S(2)}, u32[]{:S(2)}) async-start(bf16[8,160,2048]{2,1,0:T(8,128)(2,1)} %broadcast_select_fusion), calls=%async_computation | async-start | bytes 10485760 | tf_op jit(solution)/shard_map/all_to_all | solution.py:44
  81.0 47.5 %all-gather.5.cloned.1.call-start = ((), (), s32[]{:S(2)}) async-start(), calls=%async_computation.9 | async-start | bytes 2621440 | tf_op jit(solution)/shard_map/all_gather | solution.py:76
  146.8 65.2 %all-to-all-start.2 = ((bf16[8,160,2048]{2,1,0:T(8,128)(2,1)}), bf16[8,160,2048]{2,1,0:T(8,128)(2,1)}, u32[]{:S(2)}, u32[]{:S(2)}) async-start(bf16[8,160,2048]{2,1,0:T(8,128)(2,1)} %fusion.4), calls=%async_computation.3 | async-start | bytes 10485760 | tf_op jit(solution)/shard_map/all_to_all | solution.py:78
  151.7 7.3 %copy-start.3 = (bf16[1,2048,768]{2,1,0:T(8,128)(2,1)S(1)}, bf16[1,2048,768]{2,1,0:T(8,128)(2,1)}, u32[]{:S(2)}) copy-start(bf16[1,2048,768]{2,1,0:T(8,128)(2,1)} %param.12) | copy-start | bytes 9437188
  158.9 7.6 %copy-start.5 = (f32[1280,768]{1,0:T(8,128)}, f32[1280,768]{1,0:T(8,128)S(1)}, u32[]{:S(2)}) copy-start(f32[1280,768]{1,0:T(8,128)S(1)} %fusion.14) | copy-start | bytes 11796484
  166.6 1.9 copy-start.8
  212.0 65.0 %all-to-all-start.1 = ((bf16[8,160,2048]{2,1,0:T(8,128)(2,1)}), bf16[8,160,2048]{2,1,0:T(8,128)(2,1)}, u32[]{:S(2)}, u32[]{:S(2)}) async-start(bf16[8,160,2048]{2,1,0:T(8,128)(2,1)} %bitcast.51), calls=%async_computation.1 | async-start | bytes 10485760 | tf_op jit(solution)/shard_map/all_to_all | solution.py:65
  216.7 8.3 %copy-start.2 = (bf16[1,2048,768]{2,1,0:T(8,128)(2,1)S(1)}, bf16[1,2048,768]{2,1,0:T(8,128)(2,1)}, u32[]{:S(2)}) copy-start(bf16[1,2048,768]{2,1,0:T(8,128)(2,1)} %param.11) | copy-start | bytes 9437188
  216.7 8.3 %copy-start.6 = (f32[1280,768]{1,0:T(8,128)S(1)}, f32[1280,768]{1,0:T(8,128)}, u32[]{:S(2)}) copy-start(f32[1280,768]{1,0:T(8,128)} %copy-done.5) | copy-start | bytes 11796484
  216.7 8.3 %copy-start.9 = (f32[1280,768]{1,0:T(8,128)S(1)}, f32[1280,768]{1,0:T(8,128)}, u32[]{:S(2)}) copy-start(f32[1280,768]{1,0:T(8,128)} %copy-done.8) | copy-start | bytes 11796484
  223.1 1.9 copy-start.7
  225.0 9.2 %copy-start.4 = (bf16[1,2048,768]{2,1,0:T(8,128)(2,1)S(1)}, bf16[1,2048,768]{2,1,0:T(8,128)(2,1)}, u32[]{:S(2)}) copy-start(bf16[1,2048,768]{2,1,0:T(8,128)(2,1)} %param.12) | copy-start | bytes 9437188
  277.0 65.0 %all-to-all-start.3 = ((bf16[8,160,2048]{2,1,0:T(8,128)(2,1)}), bf16[8,160,2048]{2,1,0:T(8,128)(2,1)}, u32[]{:S(2)}, u32[]{:S(2)}) async-start(bf16[8,160,2048]{2,1,0:T(8,128)(2,1)} %bitcast.50), calls=%async_computation.4 | async-start | bytes 10485760 | tf_op jit(solution)/shard_map/all_to_all | solution.py:107
  281.7 87.7 %reduce-scatter.8.cloned.1.call-start = ((), (), s32[]{:S(2)}) async-start(), calls=%async_computation.11 | async-start | bytes 163840 | tf_op jit(solution)/shard_map/reduce_scatter | solution.py:128
  297.6 74.2 %reduce-scatter.4.cloned.1.call-start = ((), (), s32[]{:S(2)}) async-start(), calls=%async_computation.8 | async-start | bytes 2621440 | tf_op jit(solution)/shard_map/reduce_scatter | solution.py:67
  325.3 89.1 %reduce-scatter.6.cloned.1.call-start = ((), (), s32[]{:S(2)}) async-start(), calls=%async_computation.10 | async-start | bytes 2621440 | tf_op jit(solution)/shard_map/reduce_scatter | solution.py:119
Sparse Core Ops, SparseCore 0:
  9.6 48.6 all-gather.2
  83.4 45.0 all-gather.4
  297.7 18.3 reduce-scatter.7
  325.4 43.0 reduce-scatter.3
  371.2 43.1 reduce-scatter.5
where the time goes:
time: 430 us; the launch traced here: 421 us
  waiting for transfers between devices  182 us (42%)
  other arithmetic  86.4 us (20%)
  local copies, waits for them, and re-layouts  71.8 us (17%)
  matrix products  46.6 us (11%)
  starting transfers between devices  19.6 us (5%)
  between operations  14.6 us (3%)
    reduce_scatter x2, waiting for transfers between devices, shards(): lax.psum_scatter(jnp.zeros((col_tokens, width), jnp.float32).at[slot_toke...  42.6 us
    all_to_all x1, waiting for transfers between devices, shards(): lax.all_to_all(scaled.astype(jnp.bfloat16).reshape(col_count, capacity, w...  37.5 us
    all_gather x1, waiting for transfers between devices, shards(): cot_column = lax.all_gather(cotangent, 'dp', axis=0, tiled=True)  37.4 us
    all_to_all x1, waiting for transfers between devices, shards(): lax.all_to_all(expert_out, 'expert', split_axis=0, concat_axis=0, tiled=T...  32.7 us
    scatter-add x1, other arithmetic, shards(): out_sum = lax.psum_scatter(jnp.zeros((col_tokens, width), jnp.float32).at...  23.8 us
    scatter-add x1, other arithmetic, shards(): grad_sum = lax.psum_scatter(jnp.zeros((col_tokens, width), jnp.float32).a...  23.4 us
    all_to_all x1, waiting for transfers between devices, shards(): lax.all_to_all(input_rows.reshape(col_count, capacity, width), 'expert',...  16.5 us
    scatter x1, local copies, waits for them, and re-layouts, shards(): slot_row = jnp.zeros((slot_count + 1,), jnp.int32).at[target].set(jnp.ara...  15.5 us
  transfers between devices with their start and end apart: 9, of which 6 were waited for; matrix products, arithmetic and copies ran while one was open for 43% of the time, Pallas kernels for 0%

commit v1 on v0

v1 whole, which is shorter than its diff:
```python
import jax
import jax.numpy as jnp
from jax import lax
from jax.sharding import PartitionSpec as P

BF = jnp.bfloat16
F32 = jnp.float32
PIECES = 2
NT = (((1,), (1,)), ((), ()))


def shards(tokens, cotangent, expert_ids, router_probs, w_gate, w_up, w_down):
    cols = lax.axis_size("expert")
    groups = lax.axis_size("dp")
    group = lax.axis_index("dp")
    own, width = tokens.shape
    col_tok, top = expert_ids.shape
    capacity = col_tok * top * 5 // (4 * cols * groups)
    piece = width // PIECES
    cuts = [slice(h * piece, (h + 1) * piece) for h in range(PIECES)]

    def exchange(rows):
        return lax.all_to_all(rows, "expert", split_axis=0, concat_axis=0, tiled=True)

    def gather(rows):
        return lax.all_gather(rows, "dp", axis=0, tiled=True)

    def scatter(rows):
        return lax.psum_scatter(rows, "dp", scatter_dimension=0, tiled=True)

    tok_col = [gather(tokens[:, s]) for s in cuts]
    cot_col = [gather(cotangent[:, s]) for s in cuts]

    weights = router_probs / jnp.sum(router_probs, axis=1, keepdims=True)
    experts = jnp.arange(cols, dtype=jnp.int32) * groups + group
    named = expert_ids[None, :, :] == experts[:, None, None]
    hit = jnp.any(named, axis=2)
    slot_w = jnp.sum(jnp.where(named, weights[None], 0.0), axis=2)
    step = jnp.arange(col_tok, dtype=jnp.int32)
    before = (step[:, None] < step[None, :]).astype(BF)
    place = jnp.dot(hit.astype(BF), before, preferred_element_type=F32).astype(jnp.int32)
    place = jnp.where(hit, place, -1)
    pick = place[:, None, :] == jnp.arange(capacity, dtype=jnp.int32)[None, :, None]
    row_w = jnp.sum(jnp.where(pick, slot_w[:, None, :], 0.0), axis=2).reshape(-1, 1)
    pick_w = jnp.where(pick, slot_w[:, None, :], 0.0).astype(BF).reshape(cols * capacity, col_tok)
    pick = pick.astype(BF).reshape(cols * capacity, col_tok)

    def select(rows):
        return jnp.dot(pick, rows, preferred_element_type=F32).astype(BF)

    def send(rows):
        return exchange(rows.reshape(cols, capacity, -1)).reshape(cols * capacity, -1)

    def combine(matrix, rows):
        return lax.dot_general(
            matrix, rows, (((0,), (0,)), ((), ())), preferred_element_type=F32
        ).astype(BF)

    gate_m, up_m, down_m = w_gate[0], w_up[0], w_down[0]
    x = [send(select(c)) for c in tok_col]
    cot_sel = [select(c) for c in cot_col]
    cot = [send((row_w * c.astype(F32)).astype(BF)) for c in cot_sel]

    gate = sum(jnp.dot(r, gate_m[s], preferred_element_type=F32) for r, s in zip(x, cuts))
    up = sum(jnp.dot(r, up_m[s], preferred_element_type=F32) for r, s in zip(x, cuts))
    sig = jax.nn.sigmoid(gate)
    hidden = (gate * sig * up).astype(BF)
    back = [
        send(jnp.dot(hidden, down_m[:, s], preferred_element_type=F32).astype(BF)) for s in cuts
    ]
    out_sum = jnp.concatenate([scatter(combine(pick_w, b)) for b in back], axis=1)

    hg = sum(
        lax.dot_general(r, down_m[:, s], NT, preferred_element_type=F32) for r, s in zip(cot, cuts)
    )
    gate_grad = (hg * up * sig * (1.0 + gate * (1.0 - sig))).astype(BF)
    up_grad = (hg * gate * sig).astype(BF)

    slot_g = sum(
        jnp.sum(c.astype(F32) * b.astype(F32), axis=1) for c, b in zip(cot_sel, back)
    ).reshape(cols, capacity)
    slot_t = jnp.sum(
        jnp.where(pick.reshape(cols, capacity, col_tok) > 0, slot_g[:, :, None], 0.0), axis=1
    )
    slot_tk = jnp.sum(jnp.where(named, slot_t[:, :, None], 0.0), axis=0)
    slot_sum = scatter(slot_tk.astype(BF)).astype(F32)

    grads = [
        send(
            (
                lax.dot_general(gate_grad, gate_m[s], NT, preferred_element_type=F32)
                + lax.dot_general(up_grad, up_m[s], NT, preferred_element_type=F32)
            ).astype(BF)
        )
        for s in cuts
    ]
    grad_sum = jnp.concatenate([scatter(combine(pick, g)) for g in grads], axis=1)

    own_probs = lax.dynamic_slice_in_dim(router_probs, group * own, own, 0)
    own_total = jnp.sum(own_probs, axis=1, keepdims=True)
    own_w = own_probs / own_total
    prob_grad = (slot_sum - jnp.sum(own_w * slot_sum, axis=1, keepdims=True)) / own_total
    return out_sum, grad_sum, prob_grad


def solution(mesh):
    rows = P(("expert", "dp"), None)
    mats = P(("expert", "dp"), None, None)
    return jax.shard_map(
        shards,
        mesh=mesh,
        in_specs=(rows, rows, P("expert", None), P("expert", None), mats, mats, mats),
        out_specs=(rows, rows, rows),
        check_vma=False,
    )
```

time: 430 us -> 428 us (level)
  other arithmetic: 86.4 us -> 11.8 us
  local copies, waits for them, and re-layouts: 71.8 us -> 6.64 us
  matrix products: 46.6 us -> 94.8 us
  waiting for transfers between devices: 182 us -> 227 us
  blocking collectives: 0 us -> 35.4 us
  starting transfers between devices: 19.6 us -> 29.7 us
    scatter-add x3 -> x0, other arithmetic: 56.5 us -> none  [the longest x1 23.8 us: shards(): out_sum = lax.psum_scatter(jnp.zeros((col_tokens, width), jnp.float32).at...]
    dot_general x6 -> x21, matrix products: 46.6 us -> 94.8 us  [the longest x4 18.1 us: select(): return jnp.dot(pick, rows, preferred_element_type=F32).astype(BF)]
    all_to_all x0 -> x1, blocking collectives: none -> 35.4 us  [exchange(): lax.all_to_all(rows, 'expert', split_axis=0, concat_axis=0, tiled=True)]
    all_gather x2 -> x4, waiting for transfers between devices: 51.7 us -> 86 us  [gather(): return lax.all_gather(rows, 'dp', axis=0, tiled=True)]
    gather x3 -> x0, local copies, waits for them, and re-layouts: 32.5 us -> none  [the longest x1 12.7 us: shards(): scaled = slot_weight[:, None] * cot_column[slot_token].astype(jnp.float32)]
    all_to_all x4 -> x7, waiting for transfers between devices: 86.7 us -> 118 us  [exchange(): lax.all_to_all(rows, 'expert', split_axis=0, concat_axis=0, tiled=True)]
    scatter x2 -> x0, local copies, waits for them, and re-layouts: 31 us -> none  [the longest x1 15.5 us: shards(): slot_row = jnp.zeros((slot_count + 1,), jnp.int32).at[target].set(jnp.ara...]
    reduce_scatter x3 -> x4, waiting for transfers between devices: 42.6 us -> 21.6 us  [scatter(): return lax.psum_scatter(rows, 'dp', scatter_dimension=0, tiled=True)]
  transfers between devices with their start and end apart: 9 -> 16, of which waited for: 6 -> 10; matrix products, arithmetic and copies ran while one was open for 43% -> 18% of each run, Pallas kernels for 0% -> 0%
where the time goes in v1:
time: 428 us; the launch traced here: 420 us
  waiting for transfers between devices  227 us (53%)
  matrix products  94.8 us (22%)
  blocking collectives  35.4 us (8%)
  starting transfers between devices  29.7 us (7%)
  between operations  14.6 us (3%)
  other arithmetic  11.8 us (3%)
  local copies, waits for them, and re-layouts  6.64 us (2%)
    all_to_all x7, waiting for transfers between devices, exchange(): lax.all_to_all(rows, 'expert', split_axis=0, concat_axis=0, tiled=True)  118 us
    all_gather x4, waiting for transfers between devices, gather(): return lax.all_gather(rows, 'dp', axis=0, tiled=True)  86 us
    all_to_all x1, blocking collectives, exchange(): lax.all_to_all(rows, 'expert', split_axis=0, concat_axis=0, tiled=True)  35.4 us
    all_to_all x7, starting transfers between devices, exchange(): lax.all_to_all(rows, 'expert', split_axis=0, concat_axis=0, tiled=True)  28.9 us
    reduce_scatter x4, waiting for transfers between devices, scatter(): return lax.psum_scatter(rows, 'dp', scatter_dimension=0, tiled=True)  21.6 us
    dot_general x4, matrix products, select(): return jnp.dot(pick, rows, preferred_element_type=F32).astype(BF)  18.1 us
    dot_general x2, matrix products, shards(): lax.dot_general(r, down_m[:, s], NT, preferred_element_type=F32)  15.6 us
    dot_general x4, matrix products, combine(): lax.dot_general(matrix, rows, (((0,), (0,)), ((), ())), preferred_element...  13.7 us
  transfers between devices with their start and end apart: 16, of which 10 were waited for; matrix products, arithmetic and copies ran while one was open for 18% of the time, Pallas kernels for 0%

profile of v1, /device:TPU:0, one launch (start us, length us, event | category | flops | bytes accessed | tf_op | source)
XLA Modules:
  0.0 420.1 jit_solution(12829422802166941576)
XLA Ops:
  10.6 30.2 %all-gather.5.cloned.1.call-done = bf16[512,1024]{1,0:T(8,128)(2,1)} async-done(((bf16[128,1024]{1,0:T(8,128)(2,1)}), bf16[512,1024]{1,0:T(8,128)(2,1)}) %all-gather.5.cloned.1.call-update) | async-done | bytes 1048592 | tf_op jit(solution)/shard_map/all_gather | solution.py:26
  40.8 4.2 %convolution_convert_fusion.3 = bf16[1280,1024]{1,0:T(8,128)(2,1)} fusion(pred[1280,512]{1,0:T(32,128)(4,1)S(1)} %bitcast_compare_fusion, bf16[512,1024]{1,0:T(8,128)(2,1)} %all-gather.5.cloned.1.call-done), kind=kOutput, calls=%fused_computation.20 | convolution fusion | flops 1343488000 | bytes 4325376 | tf_op jit(solution)/shard_map/dot_general | solution.py:49
  49.5 30.2 %all-gather.7.cloned.1.call-done = bf16[512,1024]{1,0:T(8,128)(2,1)} async-done(((bf16[128,1024]{1,0:T(8,128)(2,1)}), bf16[512,1024]{1,0:T(8,128)(2,1)}) %all-gather.7.cloned.1.call-update) | async-done | bytes 1048592 | tf_op jit(solution)/shard_map/all_gather | solution.py:26
  79.7 4.3 %convolution_convert_fusion.2 = bf16[1280,1024]{1,0:T(8,128)(2,1)} fusion(pred[1280,512]{1,0:T(32,128)(4,1)S(1)} %bitcast_compare_fusion, bf16[512,1024]{1,0:T(8,128)(2,1)} %all-gather.7.cloned.1.call-done), kind=kOutput, calls=%fused_computation.19 | convolution fusion | flops 1343488000 | bytes 4325376 | tf_op jit(solution)/shard_map/dot_general | solution.py:49
  84.0 4.6 %all-to-all-start.1 = ((bf16[8,160,1024]{2,1,0:T(8,128)(2,1)}), bf16[8,160,1024]{2,1,0:T(8,128)(2,1)}, u32[]{:S(2)}, u32[]{:S(2)}) async-start(bf16[8,160,1024]{2,1,0:T(8,128)(2,1)} %bitcast.85), calls=%async_computation.1 | async-start | bytes 5242880 | tf_op jit(solution)/shard_map/all_to_all | solution.py:23
  88.7 5.6 %fusion.19 = f32[1280,768]{1,0:T(8,128)} fusion(bf16[1280,1024]{1,0:T(8,128)(2,1)S(1)} %bitcast.79, bf16[1,2048,768]{2,1,0:T(8,128)(2,1)} %param.11), kind=kOutput, calls=%fused_computation.47 | convolution fusion | flops 2013265920 | bytes 8126464 | tf_op jit(solution)/shard_map/dot_general | solution.py:64
  94.3 4.1 fusion.12
  98.4 22.6 %all-to-all-done.1 = bf16[8,160,1024]{2,1,0:T(8,128)(2,1)} async-done(((bf16[8,160,1024]{2,1,0:T(8,128)(2,1)}), bf16[8,160,1024]{2,1,0:T(8,128)(2,1)}, u32[]{:S(2)}, u32[]{:S(2)}) %all-to-all-start.1) | async-done | bytes 2621472 | tf_op jit(solution)/shard_map/all_to_all | solution.py:23
  120.9 5.8 %convolution_add_fusion.2 = f32[1280,768]{1,0:T(8,128)S(1)} fusion(f32[1280,768]{1,0:T(8,128)} %fusion.19, bf16[1280,1024]{1,0:T(8,128)(2,1)} %bitcast.5, bf16[1,2048,768]{2,1,0:T(8,128)(2,1)} %param.11), kind=kOutput, calls=%fused_computation.16 | convolution fusion | flops 2014248960 | bytes 12058624 | tf_op jit(solution)/shard_map/dot_general | solution.py:64
  126.8 7.9 %multiply_convert_fusion.2 = (bf16[1280,768]{1,0:T(8,128)(2,1)S(1)}, f32[1280,768]{1,0:T(8,128)}) fusion(f32[1280,768]{1,0:T(8,128)S(1)} %convolution_add_fusion.2, f32[1280,768]{1,0:T(8,128)S(1)} %copy-done.9, bf16[1280,1024]{1,0:T(8,128)(2,1)} %bitcast.5, bf16[1,2048,768]{2,1,0:T(8,128)(2,1)S(1)} %copy-done.5), kind=kOutput, calls=%fused_computation.12 | convolution fusion | flops 2020147200 | bytes 17956864 | tf_op jit(solution)/shard_map/dot_general | solution.py:65
  134.7 3.8 convolution_convert_fusion.5
  144.1 5.8 %convolution_convert_fusion.4 = bf16[1280,1024]{1,0:T(8,128)(2,1)} fusion(bf16[1280,768]{1,0:T(8,128)(2,1)} %copy-done.13, bf16[768,2048]{1,0:T(8,128)(2,1)} %bitcast.86), kind=kOutput, calls=%fused_computation.21 | convolution fusion | flops 2014576640 | bytes 6160384 | tf_op jit(solution)/shard_map/dot_general | solution.py:69
  149.9 24.5 %all-to-all-done.2 = bf16[8,160,1024]{2,1,0:T(8,128)(2,1)S(1)} async-done(((bf16[8,160,1024]{2,1,0:T(8,128)(2,1)}), bf16[8,160,1024]{2,1,0:T(8,128)(2,1)S(1)}, u32[]{:S(2)}, u32[]{:S(2)}) %all-to-all-start.2) | async-done | bytes 2621472 | tf_op jit(solution)/shard_map/all_to_all | solution.py:23
  174.4 4.6 %all-to-all-start.3 = ((bf16[8,160,1024]{2,1,0:T(8,128)(2,1)}), bf16[8,160,1024]{2,1,0:T(8,128)(2,1)}, u32[]{:S(2)}, u32[]{:S(2)}) async-start(bf16[8,160,1024]{2,1,0:T(8,128)(2,1)} %bitcast.78), calls=%async_computation.4 | async-start | bytes 5242880 | tf_op jit(solution)/shard_map/all_to_all | solution.py:23
  179.6 4.3 %fusion.1 = (f32[1280]{0:T(1024)S(1)}, bf16[1280,1024]{1,0:T(8,128)(2,1)}) fusion(bf16[8,160,1024]{2,1,0:T(8,128)(2,1)S(1)} %all-to-all-done.2, pred[1280,512]{1,0:T(32,128)(4,1)S(1)} %bitcast_compare_fusion, bf16[512,1024]{1,0:T(8,128)(2,1)} %all-gather.9.cloned.1.call-done), kind=kOutput, calls=%fused_computation.5 | convolution fusion | flops 1348729600 | bytes 6951936 | tf_op jit(solution)/shard_map/dot_general | solution.py:49
  183.9 25.6 %all-gather.11.cloned.1.call-done = bf16[512,1024]{1,0:T(8,128)(2,1)} async-done(((bf16[128,1024]{1,0:T(8,128)(2,1)}), bf16[512,1024]{1,0:T(8,128)(2,1)}) %all-gather.11.cloned.1.call-update) | async-done | bytes 1048592 | tf_op jit(solution)/shard_map/all_gather | solution.py:26
  211.2 5.2 %fusion.3 = (f32[1280]{0:T(1024)S(1)}, bf16[1280,1024]{1,0:T(8,128)(2,1)}) fusion(bf16[8,160,1024]{2,1,0:T(8,128)(2,1)} %all-to-all-done.3, pred[1280,512]{1,0:T(32,128)(4,1)S(1)} %bitcast_compare_fusion, bf16[512,1024]{1,0:T(8,128)(2,1)} %all-gather.11.cloned.1.call-done), kind=kOutput, calls=%fused_computation.7 | convolution fusion | flops 1348729600 | bytes 6951936 | tf_op jit(solution)/shard_map/dot_general | solution.py:49
  217.7 5.0 %fusion.2 = (bf16[1280,1024]{1,0:T(8,128)(2,1)}, bf16[1280,1024]{1,0:T(8,128)(2,1)S(1)}) fusion(bf16[1280,1024]{1,0:T(8,128)(2,1)} %get-tuple-element.18, f32[1280]{0:T(1024)S(1)} %mul.62, bf16[1280,1024]{1,0:T(8,128)(2,1)} %get-tuple-element.16), kind=kLoop, calls=%fused_computation.6 | loop fusion | flops 7864320 | bytes 10490880 | tf_op jit(solution)/shard_map/convert_element_type | solution.py:62
  222.7 35.4 %all_to_all.40 = bf16[8,160,1024]{2,1,0:T(8,128)(2,1)} all-to-all(bf16[8,160,1024]{2,1,0:T(8,128)(2,1)S(1)} %bitcast.77), channel_id=1, replica_groups=mesh['expert'=8,'dp'=4] {'expert'}, dimensions={0} | all-to-all | bytes 5242880 | tf_op jit(solution)/shard_map/all_to_all | solution.py:23
  258.1 4.4 %all-to-all-start.5 = ((bf16[8,160,1024]{2,1,0:T(8,128)(2,1)}), bf16[8,160,1024]{2,1,0:T(8,128)(2,1)}, u32[]{:S(2)}, u32[]{:S(2)}) async-start(bf16[8,160,1024]{2,1,0:T(8,128)(2,1)} %bitcast.16), calls=%async_computation.7 | async-start | bytes 5242880 | tf_op jit(solution)/shard_map/all_to_all | solution.py:23
  263.4 4.3 %bitcast_convert_fusion.2 = bf16[512,1024]{1,0:T(8,128)(2,1)} fusion(bf16[8,160,1024]{2,1,0:T(8,128)(2,1)} %all-to-all-done.3, f32[8,512]{1,0:T(8,128)S(1)} %get-tuple-element.4, s32[8,512]{1,0:T(8,128)S(1)} %fusion.42), kind=kOutput, calls=%fused_computation.33 | convolution fusion | flops 1344012288 | bytes 3702784 | tf_op jit(solution)/shard_map/dot_general | solution.py:55
  267.7 6.4 %fusion.23 = f32[1280,768]{1,0:T(8,128)} fusion(bf16[1280,1024]{1,0:T(8,128)(2,1)} %bitcast.81, bf16[768,2048]{1,0:T(8,128)(2,1)} %bitcast.87), kind=kOutput, calls=%fused_computation.51 | convolution fusion | flops 2013265920 | bytes 8126464 | tf_op jit(solution)/shard_map/dot_general | solution.py:74
  274.1 20.7 %all-to-all-done.5 = bf16[8,160,1024]{2,1,0:T(8,128)(2,1)} async-done(((bf16[8,160,1024]{2,1,0:T(8,128)(2,1)}), bf16[8,160,1024]{2,1,0:T(8,128)(2,1)}, u32[]{:S(2)}, u32[]{:S(2)}) %all-to-all-start.5) | async-done | bytes 2621472 | tf_op jit(solution)/shard_map/all_to_all | solution.py:23
  294.8 9.2 %multiply_convert_fusion = (bf16[1280,768]{1,0:T(8,128)(2,1)S(1)}, bf16[1280,768]{1,0:T(8,128)(2,1)S(1)}) fusion(f32[1280,768]{1,0:T(8,128)} %copy-done.8, f32[1280,768]{1,0:T(8,128)} %get-tuple-element.14, f32[1280,768]{1,0:T(8,128)} %fusion.23, bf16[1280,1024]{1,0:T(8,128)(2,1)} %bitcast.17, bf16[768,2048]{1,0:T(8,128)(2,1)} %bitcast.88), kind=kOutput, calls=%fused_computation.10 | convolution fusion | flops 2027028480 | bytes 19922944 | tf_op jit(solution)/shard_map/dot_general | solution.py:74
  307.3 3.8 add_convert_fusion
  311.1 4.4 %all-to-all-start.7 = ((bf16[8,160,1024]{2,1,0:T(8,128)(2,1)}), bf16[8,160,1024]{2,1,0:T(8,128)(2,1)}, u32[]{:S(2)}, u32[]{:S(2)}) async-start(bf16[8,160,1024]{2,1,0:T(8,128)(2,1)} %bitcast.82), calls=%async_computation.10 | async-start | bytes 5242880 | tf_op jit(solution)/shard_map/all_to_all | solution.py:23
  318.4 4.4 %fusion.17 = f32[1280,1024]{1,0:T(8,128)S(1)} fusion(bf16[1280,768]{1,0:T(8,128)(2,1)} %copy-done.10, bf16[1,2048,768]{2,1,0:T(8,128)(2,1)} %param.11), kind=kOutput, calls=%fused_computation.45 | convolution fusion | flops 2013265920 | bytes 8781824 | tf_op jit(solution)/shard_map/dot_general | solution.py:91
  322.8 3.8 add_convert_fusion.1
  326.7 21.2 %all-to-all-done.7 = bf16[8,160,1024]{2,1,0:T(8,128)(2,1)} async-done(((bf16[8,160,1024]{2,1,0:T(8,128)(2,1)}), bf16[8,160,1024]{2,1,0:T(8,128)(2,1)}, u32[]{:S(2)}, u32[]{:S(2)}) %all-to-all-start.7) | async-done | bytes 2621472 | tf_op jit(solution)/shard_map/all_to_all | solution.py:23
  351.5 4.3 %bitcast_convert_fusion = bf16[512,1024]{1,0:T(8,128)(2,1)} fusion(bf16[8,160,1024]{2,1,0:T(8,128)(2,1)} %all-to-all-done.7, s32[8,512]{1,0:T(8,128)S(1)} %fusion.42), kind=kOutput, calls=%fused_computation.31 | convolution fusion | flops 1343356928 | bytes 3686400 | tf_op jit(solution)/shard_map/dot_general | solution.py:55
  355.9 27.7 %all-to-all-done.6 = bf16[8,160,1024]{2,1,0:T(8,128)(2,1)S(1)} async-done(((bf16[8,160,1024]{2,1,0:T(8,128)(2,1)}), bf16[8,160,1024]{2,1,0:T(8,128)(2,1)S(1)}, u32[]{:S(2)}, u32[]{:S(2)}) %all-to-all-start.6) | async-done | bytes 2621472 | tf_op jit(solution)/shard_map/all_to_all | solution.py:23
  389.6 21.6 %reduce-scatter.12.cloned.1.call-done = bf16[128,1024]{1,0:T(8,128)(2,1)} async-done(((bf16[512,1024]{1,0:T(8,128)(2,1)}), bf16[128,1024]{1,0:T(8,128)(2,1)}) %reduce-scatter.12.cloned.1.call-update) | async-done | bytes 262160 | tf_op jit(solution)/shard_map/reduce_scatter | solution.py:29
  (82 shorter events, 35.6 us)
Async XLA Ops:
  7.2 33.6 %all-gather.5.cloned.1.call-start = ((), (), s32[]{:S(2)}) async-start(), calls=%async_computation.13 | async-start | bytes 1310720 | tf_op jit(solution)/shard_map/all_gather | solution.py:26
  45.1 39.0 %all-to-all-start = ((bf16[8,160,1024]{2,1,0:T(8,128)(2,1)}), bf16[8,160,1024]{2,1,0:T(8,128)(2,1)S(1)}, u32[]{:S(2)}, u32[]{:S(2)}) async-start(bf16[8,160,1024]{2,1,0:T(8,128)(2,1)} %bitcast.83), calls=%async_computation | async-start | bytes 5242880 | tf_op jit(solution)/shard_map/all_to_all | solution.py:23
  48.7 31.0 %all-gather.7.cloned.1.call-start = ((), (), s32[]{:S(2)}) async-start(), calls=%async_computation.14 | async-start | bytes 1310720 | tf_op jit(solution)/shard_map/all_gather | solution.py:26
  84.0 36.9 %all-to-all-start.1 = ((bf16[8,160,1024]{2,1,0:T(8,128)(2,1)}), bf16[8,160,1024]{2,1,0:T(8,128)(2,1)}, u32[]{:S(2)}, u32[]{:S(2)}) async-start(bf16[8,160,1024]{2,1,0:T(8,128)(2,1)} %bitcast.85), calls=%async_computation.1 | async-start | bytes 5242880 | tf_op jit(solution)/shard_map/all_to_all | solution.py:23
  88.6 5.6 %copy-start.4 = (bf16[1,2048,768]{2,1,0:T(8,128)(2,1)S(1)}, bf16[1,2048,768]{2,1,0:T(8,128)(2,1)}, u32[]{:S(2)}) copy-start(bf16[1,2048,768]{2,1,0:T(8,128)(2,1)} %param.12) | copy-start | bytes 9437188
  120.9 5.8 %copy-start.5 = (bf16[1,2048,768]{2,1,0:T(8,128)(2,1)S(1)}, bf16[1,2048,768]{2,1,0:T(8,128)(2,1)}, u32[]{:S(2)}) copy-start(bf16[1,2048,768]{2,1,0:T(8,128)(2,1)} %param.12) | copy-start | bytes 9437188
  120.9 5.8 %copy-start.9 = (f32[1280,768]{1,0:T(8,128)S(1)}, f32[1280,768]{1,0:T(8,128)}, u32[]{:S(2)}) copy-start(f32[1280,768]{1,0:T(8,128)} %fusion.12) | copy-start | bytes 11796484
  126.8 7.9 %copy-start.8 = (f32[1280,768]{1,0:T(8,128)}, f32[1280,768]{1,0:T(8,128)S(1)}, u32[]{:S(2)}) copy-start(f32[1280,768]{1,0:T(8,128)S(1)} %convolution_add_fusion.2) | copy-start | bytes 11796484
  126.8 7.9 %copy-start.2 = (bf16[1,768,2048]{2,1,0:T(8,128)(2,1)S(1)}, bf16[1,768,2048]{2,1,0:T(8,128)(2,1)}, u32[]{:S(2)}) copy-start(bf16[1,768,2048]{2,1,0:T(8,128)(2,1)} %param.13) | copy-start | bytes 9437188
  134.7 3.8 copy-start.13
  138.5 35.8 %all-to-all-start.2 = ((bf16[8,160,1024]{2,1,0:T(8,128)(2,1)}), bf16[8,160,1024]{2,1,0:T(8,128)(2,1)S(1)}, u32[]{:S(2)}, u32[]{:S(2)}) async-start(bf16[8,160,1024]{2,1,0:T(8,128)(2,1)} %bitcast.84), calls=%async_computation.2 | async-start | bytes 5242880 | tf_op jit(solution)/shard_map/all_to_all | solution.py:23
  142.2 37.4 %all-gather.9.cloned.1.call-start = ((), (), s32[]{:S(2)}) async-start(), calls=%async_computation.17 | async-start | bytes 1310720 | tf_op jit(solution)/shard_map/all_gather | solution.py:26
  174.4 5.2 %copy-start = (f32[512,8]{0,1:T(8,128)S(1)}, f32[512,8]{0,1:T(8,128)}, u32[]{:S(2)}) copy-start(f32[512,8]{0,1:T(8,128)} %param.10) | copy-start | bytes 49156
  174.4 36.9 %all-to-all-start.3 = ((bf16[8,160,1024]{2,1,0:T(8,128)(2,1)}), bf16[8,160,1024]{2,1,0:T(8,128)(2,1)}, u32[]{:S(2)}, u32[]{:S(2)}) async-start(bf16[8,160,1024]{2,1,0:T(8,128)(2,1)} %bitcast.78), calls=%async_computation.4 | async-start | bytes 5242880 | tf_op jit(solution)/shard_map/all_to_all | solution.py:23
  178.9 30.6 %all-gather.11.cloned.1.call-start = ((), (), s32[]{:S(2)}) async-start(), calls=%async_computation.18 | async-start | bytes 1310720 | tf_op jit(solution)/shard_map/all_gather | solution.py:26
  183.9 33.2 %copy-start.1 = (s32[512,8]{0,1:T(8,128)S(1)}, s32[512,8]{0,1:T(8,128)}, u32[]{:S(2)}) copy-start(s32[512,8]{0,1:T(8,128)} %param.9) | copy-start | bytes 49156
  258.1 36.7 %all-to-all-start.5 = ((bf16[8,160,1024]{2,1,0:T(8,128)(2,1)}), bf16[8,160,1024]{2,1,0:T(8,128)(2,1)}, u32[]{:S(2)}, u32[]{:S(2)}) async-start(bf16[8,160,1024]{2,1,0:T(8,128)(2,1)} %bitcast.16), calls=%async_computation.7 | async-start | bytes 5242880 | tf_op jit(solution)/shard_map/all_to_all | solution.py:23
  262.5 123.8 %reduce-scatter.16.cloned.1.call-start = ((), (), s32[]{:S(2)}) async-start(), calls=%async_computation.21 | async-start | bytes 163840
  263.4 124.4 %reduce-scatter.10.cloned.1.call-start = ((), (), s32[]{:S(2)}) async-start(), calls=%async_computation.16 | async-start | bytes 1310720 | tf_op jit(solution)/shard_map/reduce_scatter | solution.py:29
  294.8 9.2 %copy-start.3 = (bf16[1,2048,768]{2,1,0:T(8,128)(2,1)S(1)}, bf16[1,2048,768]{2,1,0:T(8,128)(2,1)}, u32[]{:S(2)}) copy-start(bf16[1,2048,768]{2,1,0:T(8,128)(2,1)} %param.11) | copy-start | bytes 9437188
  304.0 2.3 copy-start.10
  304.0 2.3 copy-start.11
  304.0 3.3 copy-start.6
  311.1 36.7 %all-to-all-start.7 = ((bf16[8,160,1024]{2,1,0:T(8,128)(2,1)}), bf16[8,160,1024]{2,1,0:T(8,128)(2,1)}, u32[]{:S(2)}, u32[]{:S(2)}) async-start(bf16[8,160,1024]{2,1,0:T(8,128)(2,1)} %bitcast.82), calls=%async_computation.10 | async-start | bytes 5242880 | tf_op jit(solution)/shard_map/all_to_all | solution.py:23
  315.6 72.2 %reduce-scatter.8.cloned.1.call-start = ((), (), s32[]{:S(2)}) async-start(), calls=%async_computation.15 | async-start | bytes 1310720 | tf_op jit(solution)/shard_map/reduce_scatter | solution.py:29
  318.4 4.4 %copy-start.7 = (bf16[1,2048,768]{2,1,0:T(8,128)(2,1)S(1)}, bf16[1,2048,768]{2,1,0:T(8,128)(2,1)}, u32[]{:S(2)}) copy-start(bf16[1,2048,768]{2,1,0:T(8,128)(2,1)} %param.12) | copy-start | bytes 9437188
  318.4 4.4 %copy-start.12 = (bf16[1280,768]{1,0:T(8,128)(2,1)S(1)}, bf16[1280,768]{1,0:T(8,128)(2,1)}, u32[]{:S(2)}) copy-start(bf16[1280,768]{1,0:T(8,128)(2,1)} %copy-done.11) | copy-start | bytes 5898244
  347.8 35.8 %all-to-all-start.6 = ((bf16[8,160,1024]{2,1,0:T(8,128)(2,1)}), bf16[8,160,1024]{2,1,0:T(8,128)(2,1)S(1)}, u32[]{:S(2)}, u32[]{:S(2)}) async-start(bf16[8,160,1024]{2,1,0:T(8,128)(2,1)} %bitcast.18), calls=%async_computation.8 | async-start | bytes 5242880 | tf_op jit(solution)/shard_map/all_to_all | solution.py:23
  351.5 38.2 %reduce-scatter.14.cloned.1.call-start = ((), (), s32[]{:S(2)}) async-start(), calls=%async_computation.20 | async-start | bytes 1310720 | tf_op jit(solution)/shard_map/reduce_scatter | solution.py:29
  355.9 55.4 %reduce-scatter.12.cloned.1.call-start = ((), (), s32[]{:S(2)}) async-start(), calls=%async_computation.19 | async-start | bytes 1310720 | tf_op jit(solution)/shard_map/reduce_scatter | solution.py:29
Sparse Core Ops, SparseCore 0:
  10.1 30.6 all-gather.4
  51.7 27.9 all-gather.6
  145.2 27.8 all-gather.8
  181.6 27.8 all-gather.10
  265.9 19.0 reduce-scatter.15
  287.3 25.3 reduce-scatter.9
  318.7 27.0 reduce-scatter.7
  356.0 27.0 reduce-scatter.13
  386.3 24.8 reduce-scatter.11

commit v2 on v1

--- a/solution.py
+++ b/solution.py
@@ -1,12 +1,263 @@
+import functools
+
 import jax
 import jax.numpy as jnp
 from jax import lax
+from jax.experimental import pallas as pl
+from jax.experimental.pallas import tpu as pltpu
 from jax.sharding import PartitionSpec as P
 
 BF = jnp.bfloat16
 F32 = jnp.float32
 PIECES = 2
 NT = (((1,), (1,)), ((), ()))
+CHUNKS = 4
+VMEM_BYTES = 60 * 1024 * 1024
+MESH = pl.DeviceIdType.MESH
+
+
+def layer_kernel(
+    cols, groups, tok_ref, cot_ref, pick_ref, pick_t_ref, pick_wt_ref, row_w_ref, kinv_ref,
+    gate_ref, up_ref, down_ref, out_ref, grad_ref, slot_ref,
+    tok_col, cot_col, send_tok, recv_tok, send_cot, recv_cot, ret_out, gate_keep, up_keep,
+    slot_rows, slot_col, rs_out, rs_grad, rs_slot,
+    zsend, zrecv, ssend, srecv, osend, orecv, gsend, grecv, rsend, rrecv,
+):
+    me = lax.axis_index("expert")
+    z = lax.axis_index("dp")
+    own, width = tok_ref.shape
+    cap = pick_ref.shape[0] // cols
+    part = width // CHUNKS
+    cuts = [slice(c * part, (c + 1) * part) for c in range(CHUNKS)]
+    whole = slice(0, width)
+
+    def block(index, size):
+        return pl.ds(pl.multiple_of(index * size, 16), size)
+
+    def peer(j):
+        return lax.rem(me + j, cols)
+
+    def zpeer(j):
+        return lax.rem(z + j, groups)
+
+    def loop(start, stop, body):
+        def step(j, carry):
+            body(j)
+            return carry
+        lax.fori_loop(start, stop, step, 0)
+
+    def remote(src, dst, send, recv, device):
+        return pltpu.make_async_remote_copy(
+            src_ref=src, dst_ref=dst, send_sem=send, recv_sem=recv,
+            device_id=device, device_id_type=MESH,
+        )
+
+    barrier = pltpu.get_barrier_semaphore()
+    loop(1, cols, lambda j: pl.semaphore_signal(
+        barrier, inc=1, device_id=(peer(j), z), device_id_type=MESH))
+    loop(1, groups, lambda j: pl.semaphore_signal(
+        barrier, inc=1, device_id=(me, zpeer(j)), device_id_type=MESH))
+    pl.semaphore_wait(barrier, cols + groups - 2)
+
+    def zcopy(k, c, src_z, to):
+        src = (tok_ref, cot_ref)[k]
+        dst = (tok_col, cot_col)[k]
+        return remote(src.at[:, cuts[c]], dst.at[block(src_z, own), cuts[c]],
+                      zsend.at[k, c, to], zrecv.at[k, c, src_z], (me, to))
+
+    for k in range(2):
+        for c in range(CHUNKS):
+            loop(1, groups, lambda j, k=k, c=c: zcopy(k, c, z, zpeer(j)).start())
+    tok_col[block(z, own), :] = tok_ref[...]
+    cot_col[block(z, own), :] = cot_ref[...]
+
+    def row_copy(k, c, src, to):
+        a = (send_tok, send_cot)[k]
+        b = (recv_tok, recv_cot)[k]
+        return remote(a.at[block(to, cap), cuts[c]], b.at[block(src, cap), cuts[c]],
+                      ssend.at[k, c, to], srecv.at[k, c, src], (to, z))
+
+    for k in range(2):
+        for c in range(CHUNKS):
+            loop(1, groups, lambda j, k=k, c=c: zcopy(k, c, zpeer(j), zpeer(j)).wait_recv())
+
+            def picked(d, k=k, c=c):
+                col = (tok_col, cot_col)[k]
+                rows = jnp.dot(pick_ref[block(d, cap), :], col[:, cuts[c]],
+                               preferred_element_type=F32)
+                if k == 1:
+                    rows = rows * row_w_ref[block(d, cap), :]
+                return rows.astype(BF)
+
+            def dispatch(j, k=k, c=c):
+                d = peer(j)
+                (send_tok, send_cot)[k][block(d, cap), cuts[c]] = picked(d)
+                if k == 1:
+                    row_copy(0, c, me, d).wait_send()
+                row_copy(k, c, me, d).start()
+
+            loop(1, cols, dispatch)
+            mine = picked(me)
+            (recv_tok, recv_cot)[k][block(me, cap), cuts[c]] = mine
+            if k == 1:
+                send_cot[block(me, cap), cuts[c]] = mine
+    for k in range(2):
+        for c in range(CHUNKS):
+            loop(1, groups, lambda j, k=k, c=c: zcopy(k, c, z, zpeer(j)).wait_send())
+
+    def out_copy(src, to):
+        return remote(recv_tok.at[block(to, cap), :], ret_out.at[block(src, cap), :],
+                      osend.at[to], orecv.at[src], (to, z))
+
+    def forward(s):
+        rows = block(s, cap)
+        x = recv_tok[rows, :]
+        gate = jnp.dot(x, gate_ref[...], preferred_element_type=F32)
+        up = jnp.dot(x, up_ref[...], preferred_element_type=F32)
+        gate_keep[rows, :] = gate.astype(BF)
+        up_keep[rows, :] = up.astype(BF)
+        hidden = (gate * jax.nn.sigmoid(gate) * up).astype(BF)
+        return jnp.dot(hidden, down_ref[...], preferred_element_type=F32).astype(BF)
+
+    ret_out[block(me, cap), :] = forward(me)
+
+    def forward_step(j):
+        s = peer(cols - j)
+        for c in range(CHUNKS):
+            row_copy(0, c, s, s).wait_recv()
+        recv_tok[block(s, cap), :] = forward(s)
+        out_copy(me, s).start()
+
+    loop(1, cols, forward_step)
+
+    def backward(s):
+        rows = block(s, cap)
+        hg = lax.dot_general(recv_cot[rows, :], down_ref[...], NT, preferred_element_type=F32)
+        gate = gate_keep[rows, :].astype(F32)
+        up = up_keep[rows, :].astype(F32)
+        sig = jax.nn.sigmoid(gate)
+        gate_keep[rows, :] = (hg * up * sig * (1.0 + gate * (1.0 - sig))).astype(BF)
+        up_keep[rows, :] = (hg * gate * sig).astype(BF)
+
+    backward(me)
+
+    def backward_step(j):
+        s = peer(cols - j)
+        for c in range(CHUNKS):
+            row_copy(1, c, s, s).wait_recv()
+        backward(s)
+
+    loop(1, cols, backward_step)
+
+    def grad_copy(c, src, to):
+        return remote(recv_cot.at[block(to, cap), cuts[c]], send_tok.at[block(src, cap), cuts[c]],
+                      gsend.at[c, to], grecv.at[c, src], (to, z))
+
+    def grad_rows(s, c):
+        rows = block(s, cap)
+        return (
+            lax.dot_general(gate_keep[rows, :], gate_ref[cuts[c], :], NT,
+                            preferred_element_type=F32)
+            + lax.dot_general(up_keep[rows, :], up_ref[cuts[c], :], NT,
+                              preferred_element_type=F32)
+        ).astype(BF)
+
+    for c in range(CHUNKS):
+        def grad_step(j, c=c):
+            s = peer(cols - j)
+            recv_cot[block(s, cap), cuts[c]] = grad_rows(s, c)
+            grad_copy(c, me, s).start()
+
+        loop(1, cols, grad_step)
+        send_tok[block(me, cap), cuts[c]] = grad_rows(me, c)
+
+    def sum_copy(n, src_z, to):
+        a, b, s = ((cot_col, rs_grad, cuts[n]) if n < CHUNKS else
+                   (tok_col, rs_out, whole) if n == CHUNKS else
+                   (slot_col, rs_slot, slice(0, slot_col.shape[1])))
+        return remote(a.at[block(to, own), s], b.at[block(src_z, own), s],
+                      rsend.at[n, to], rrecv.at[n, src_z], (me, to))
+
+    def send_sums(n):
+        loop(1, groups, lambda j: sum_copy(n, z, zpeer(j)).start())
+
+    def take_sums(n, a, b, dst, s):
+        total = a[block(z, own), s].astype(F32)
+        for j in range(1, groups):
+            sum_copy(n, zpeer(j), zpeer(j)).wait_recv()
+            total = total + b[block(zpeer(j), own), s].astype(F32)
+        dst[:, s] = total.astype(dst.dtype)
+
+    loop(1, cols, lambda j: out_copy(peer(j), peer(j)).wait_recv())
+    for s in cuts:
+        tok_col[:, s] = jnp.dot(pick_wt_ref[...], ret_out[:, s],
+                                preferred_element_type=F32).astype(BF)
+    send_sums(CHUNKS)
+
+    def slot_step(d):
+        rows = block(d, cap)
+        dots = jnp.sum(send_cot[rows, :].astype(F32) * ret_out[rows, :].astype(F32),
+                       axis=1, keepdims=True)
+        slot_rows[rows, :] = (dots * kinv_ref[rows, :]).astype(BF)
+
+    loop(0, cols, slot_step)
+    slot_col[...] = jnp.dot(pick_t_ref[...], slot_rows[...],
+                            preferred_element_type=F32).astype(BF)
+    send_sums(CHUNKS + 1)
+
+    for c in range(CHUNKS):
+        loop(1, cols, lambda j, c=c: grad_copy(c, peer(j), peer(j)).wait_recv())
+        cot_col[:, cuts[c]] = jnp.dot(pick_t_ref[...], send_tok[:, cuts[c]],
+                                      preferred_element_type=F32).astype(BF)
+        send_sums(c)
+    take_sums(CHUNKS, tok_col, rs_out, out_ref, whole)
+    take_sums(CHUNKS + 1, slot_col, rs_slot, slot_ref, slice(0, slot_col.shape[1]))
+    for c in range(CHUNKS):
+        take_sums(c, cot_col, rs_grad, grad_ref, cuts[c])
+
+    def finish(j):
+        for c in range(CHUNKS):
+            row_copy(1, c, me, peer(j)).wait_send()
+            grad_copy(c, me, peer(j)).wait_send()
+        out_copy(me, peer(j)).wait_send()
+
+    loop(1, cols, finish)
+    for n in range(CHUNKS + 2):
+        loop(1, groups, lambda j, n=n: sum_copy(n, z, zpeer(j)).wait_send())
+
+
+def layer(cols, groups, tokens, cotangent, pick, pick_t, pick_wt, row_w, kinv, gate_m, up_m, down_m):
+    own, width = tokens.shape
+    slots, col_tok = pick.shape
+    ff = gate_m.shape[1]
+    lanes = kinv.shape[1]
+    dma = pltpu.SemaphoreType.DMA
+    vmem = pl.BlockSpec(memory_space=pltpu.VMEM)
+    rows = pltpu.VMEM((slots, width), BF)
+    column = pltpu.VMEM((col_tok, width), BF)
+    return pl.pallas_call(
+        functools.partial(layer_kernel, cols, groups),
+        out_shape=(
+            jax.ShapeDtypeStruct((own, width), BF),
+            jax.ShapeDtypeStruct((own, width), BF),
+            jax.ShapeDtypeStruct((own, lanes), F32),
+        ),
+        in_specs=[vmem] * 10,
+        out_specs=(vmem, vmem, vmem),
+        scratch_shapes=[
+            column, column, rows, rows, rows, rows, rows,
+            pltpu.VMEM((slots, ff), BF), pltpu.VMEM((slots, ff), BF),
+            pltpu.VMEM((slots, lanes), BF), pltpu.VMEM((col_tok, lanes), BF),
+            column, column, pltpu.VMEM((col_tok, lanes), BF),
+            dma((2, CHUNKS, groups)), dma((2, CHUNKS, groups)),
+            dma((2, CHUNKS, cols)), dma((2, CHUNKS, cols)),
+            dma((cols,)), dma((cols,)),
+            dma((CHUNKS, cols)), dma((CHUNKS, cols)),
+            dma((CHUNKS + 2, groups)), dma((CHUNKS + 2, groups)),
+        ],
+        compiler_params=pltpu.CompilerParams(
+            collective_id=0, has_side_effects=True, vmem_limit_bytes=VMEM_BYTES),
+    )(tokens, cotangent, pick, pick_t, pick_wt, row_w, kinv, gate_m, up_m, down_m)
 
 
 def shards(tokens, cotangent, expert_ids, router_probs, w_gate, w_up, w_down):
@@ -27,9 +278,6 @@
 
     def scatter(rows):
         return lax.psum_scatter(rows, "dp", scatter_dimension=0, tiled=True)
-
-    tok_col = [gather(tokens[:, s]) for s in cuts]
-    cot_col = [gather(cotangent[:, s]) for s in cuts]
 
     weights = router_probs / jnp.sum(router_probs, axis=1, keepdims=True)
     experts = jnp.arange(cols, dtype=jnp.int32) * groups + group
@@ -45,6 +293,33 @@
     pick_w = jnp.where(pick, slot_w[:, None, :], 0.0).astype(BF).reshape(cols * capacity, col_tok)
     pick = pick.astype(BF).reshape(cols * capacity, col_tok)
 
+    own_probs = lax.dynamic_slice_in_dim(router_probs, group * own, own, 0)
+    own_total = jnp.sum(own_probs, axis=1, keepdims=True)
+    own_w = own_probs / own_total
+
+    def prob_grad_of(slot_sum):
+        return (slot_sum - jnp.sum(own_w * slot_sum, axis=1, keepdims=True)) / own_total
+
+    slots = cols * capacity
+    ff = w_gate.shape[2]
+    held = 2 * (5 * slots * width + 4 * col_tok * width + 3 * width * ff + 2 * slots * ff)
+    held = held + 6 * slots * col_tok
+    if held < VMEM_BYTES:
+        k_of = jnp.sum(jnp.where(named, jnp.arange(top, dtype=jnp.int32), 0), axis=2)
+        row_k = jnp.sum(
+            jnp.where(pick.reshape(cols, capacity, col_tok) > 0, k_of[:, None, :], 0), axis=2
+        ).reshape(-1, 1)
+        lanes = jnp.arange(128, dtype=jnp.int32)[None, :]
+        kinv = jnp.where((row_k == lanes) & (row_w > 0), 1.0 / jnp.maximum(row_w, 1e-30), 0.0)
+        out_sum, grad_sum, slot_sum = layer(
+            cols, groups, tokens, cotangent, pick, pick.T, pick_w.T, row_w, kinv,
+            w_gate[0], w_up[0], w_down[0])
+        return out_sum, grad_sum, prob_grad_of(slot_sum[:, :top])
+
+    tok_col = [gather(tokens[:, s]) for s in cuts]
+    cot_col = [gather(cotangent[:, s]) for s in cuts]
+
+
     def select(rows):
         return jnp.dot(pick, rows, preferred_element_type=F32).astype(BF)
 
@@ -96,11 +371,7 @@
     ]
     grad_sum = jnp.concatenate([scatter(combine(pick, g)) for g in grads], axis=1)
 
-    own_probs = lax.dynamic_slice_in_dim(router_probs, group * own, own, 0)
-    own_total = jnp.sum(own_probs, axis=1, keepdims=True)
-    own_w = own_probs / own_total
-    prob_grad = (slot_sum - jnp.sum(own_w * slot_sum, axis=1, keepdims=True)) / own_total
-    return out_sum, grad_sum, prob_grad
+    return out_sum, grad_sum, prob_grad_of(slot_sum)
 
 
 def solution(mesh):

time: 428 us -> 332 us (0.78)
  the two profiles are of different devices: /device:TPU:0 before, /device:TPU:26 now
where the time goes in v2:
time: 332 us; the launch traced here: 331 us
  Pallas kernels  302 us (91%)
  local copies, waits for them, and re-layouts  15.2 us (5%)
  other arithmetic  13.4 us (4%)
    pallas_call x1, Pallas kernels, layer(): pl.pallas_call(functools.partial(layer_kernel, cols, groups), out_shape=(...  302 us

profile of v2, /device:TPU:26, one launch (start us, length us, event | category | flops | bytes accessed | tf_op | source)
XLA Modules:
  0.0 331.1 jit_solution(17373483411029698467)
XLA Ops:
  0.6 0.8 compare_reduce_fusion
  1.5 0.2 fusion.2
  1.7 0.7 reduce_sum.63
  2.4 0.7 broadcast_divide_fusion
  3.1 0.8 fusion.5
  4.0 0.4 select_reduce_fusion.1
  4.3 0.1 div.40
  4.4 0.1 gt.24
  4.5 0.8 fusion.6
  5.3 0.5 select_reduce_fusion
  5.9 0.1 eq.64
  5.9 1.7 fusion.4.kinv_ref
  7.7 1.8 eq.56
  9.5 2.1 copy.24
  11.7 1.2 broadcast_in_dim.85
  12.8 2.4 copy.25
  15.2 0.1 eq.59
  15.3 3.0 fusion.1
  18.3 1.3 convert_bitcast_fusion
  19.5 1.5 copy.26.pick_ref
  21.0 1.3 reshape.54.row_w_ref
  22.3 301.5 %shard_map.94 = (bf16[128,2048]{1,0:T(8,128)(2,1)}, bf16[128,2048]{1,0:T(8,128)(2,1)}, f32[128,128]{1,0:T(8,128)}) custom-call(bf16[128,2048]{1,0:T(8,128)(2,1)} %tok_ref.1, bf16[128,2048]{1,0:T(8,128)(2,1)} %cot_ref.1, bf16[1280,512]{1,0:T(8,128)(2,1)} %copy.26.pick_ref, bf16[512,1280]{1,0:T(8,128)(2,1)} %get-tuple-element.22.pick_t_ref, ...), custom_call_target="tpu_custom_call" | custom-call | tf_op jit(solution)/shard_map/pallas_call | solution.py:238
  323.8 0.7 fusion.7
  324.6 0.1 copy.30
  324.7 1.0 multiply_reduce_fusion
  325.7 0.9 subtract_divide_fusion
  326.6 0.7 copy.29
  327.3 1.9 copy.34
  329.2 1.9 copy.35
  (4 shorter events, 0.0 us)

commit v3 on v2

--- a/solution.py
+++ b/solution.py
@@ -65,9 +65,12 @@
         return remote(src.at[:, cuts[c]], dst.at[block(src_z, own), cuts[c]],
                       zsend.at[k, c, to], zrecv.at[k, c, src_z], (me, to))
 
-    for k in range(2):
-        for c in range(CHUNKS):
-            loop(1, groups, lambda j, k=k, c=c: zcopy(k, c, z, zpeer(j)).start())
+    def zstart(n):
+        if n < 2 * CHUNKS:
+            loop(1, groups, lambda j: zcopy(n // CHUNKS, n % CHUNKS, z, zpeer(j)).start())
+
+    zstart(0)
+    zstart(1)
     tok_col[block(z, own), :] = tok_ref[...]
     cot_col[block(z, own), :] = cot_ref[...]
 
@@ -80,6 +83,7 @@
     for k in range(2):
         for c in range(CHUNKS):
             loop(1, groups, lambda j, k=k, c=c: zcopy(k, c, zpeer(j), zpeer(j)).wait_recv())
+            zstart(k * CHUNKS + c + 2)
 
             def picked(d, k=k, c=c):
                 col = (tok_col, cot_col)[k]

time: 332 us -> 322 us (0.970)
  the two profiles are of different devices: /device:TPU:26 before, /device:TPU:10 now
where the time goes in v3:
time: 322 us; the launch traced here: 321 us
  Pallas kernels  291 us (90%)
  local copies, waits for them, and re-layouts  15.2 us (5%)
  other arithmetic  13.4 us (4%)
    pallas_call x1, Pallas kernels, layer(): pl.pallas_call(functools.partial(layer_kernel, cols, groups), out_shape=(...  291 us

profile of v3, /device:TPU:10, one launch (start us, length us, event | category | flops | bytes accessed | tf_op | source)
XLA Modules:
  0.0 320.8 jit_solution(6206769691557389861)
XLA Ops:
  0.6 0.8 compare_reduce_fusion
  1.5 0.2 fusion.2
  1.7 0.7 reduce_sum.63
  2.4 0.7 broadcast_divide_fusion
  3.1 0.8 fusion.5
  4.0 0.4 select_reduce_fusion.1
  4.3 0.1 div.40
  4.4 0.1 gt.24
  4.5 0.8 fusion.6
  5.3 0.5 select_reduce_fusion
  5.9 0.1 eq.64
  5.9 1.7 fusion.4.kinv_ref
  7.7 1.8 eq.56
  9.5 2.1 copy.24
  11.7 1.2 broadcast_in_dim.85
  12.8 2.4 copy.25
  15.2 0.1 eq.59
  15.3 3.0 fusion.1
  18.3 1.3 convert_bitcast_fusion
  19.5 1.5 copy.26.pick_ref
  21.0 1.3 reshape.54.row_w_ref
  22.3 291.3 %shard_map.94 = (bf16[128,2048]{1,0:T(8,128)(2,1)}, bf16[128,2048]{1,0:T(8,128)(2,1)}, f32[128,128]{1,0:T(8,128)}) custom-call(bf16[128,2048]{1,0:T(8,128)(2,1)} %tok_ref.1, bf16[128,2048]{1,0:T(8,128)(2,1)} %cot_ref.1, bf16[1280,512]{1,0:T(8,128)(2,1)} %copy.26.pick_ref, bf16[512,1280]{1,0:T(8,128)(2,1)} %get-tuple-element.22.pick_t_ref, ...), custom_call_target="tpu_custom_call" | custom-call | tf_op jit(solution)/shard_map/pallas_call | solution.py:242
  313.6 0.7 fusion.7
  314.3 0.1 copy.30
  314.4 1.0 multiply_reduce_fusion
  315.4 0.9 subtract_divide_fusion
  316.4 0.7 copy.29
  317.1 1.9 copy.34
  318.9 1.9 copy.35
  (4 shorter events, 0.0 us)
